TPU v7x, 32 devices: a whole 2x2x4 slice. The times are simulated.
32 devices in a mesh: wide: 8 (over z, x), narrow: 4 (over y, core).
Axes of the slice: x: 2, y: 2, z: 4, core: 2. Of those that a mesh axis runs over, the one named last changes fastest.
Arguments:
- embeddings: bfloat16 [16384, 768], P(('wide', 'narrow')), may hold values from -6 to 6
- coarse_ids: int32 [16384, 1], P(('wide', 'narrow')), may hold values from 0 to 7; in each aligned block of 512 rows (0 to 511, 512 to 1023, ...) at most 128 rows name the same one
- fine_ids: int32 [16384], P(('wide', 'narrow')), may hold values from 0 to 2047
- centroids: bfloat16 [16384, 768], P(('wide', 'narrow')), may hold values from -6 to 6
- candidates: int32 [128, 8], P(('wide', 'narrow')), may hold values from 0 to 63, as said below
Outputs:
- new_centroids: bfloat16 [16384, 768], P(('wide', 'narrow'))
- best_score: float32 [16384], P(('wide', 'narrow'))
Inputs may be any that keep to these rules, and one draw needn't show every extreme that they name: `candidates`: counting the 32 entries of the 4 consecutive query blocks of one device, at most 8 lie among the 8 blocks of one coarse cluster, and some coarse cluster holds exactly 8 of every device's entries.
All inputs are finite; a program needn't handle non-finite values.
Results may differ from a plain program's by a relative error of at most 0.0055.
Values may be sent and summed in bfloat16 or wider, within the bound.
A program may use at most 192 MiB of HBM per device.

v0:
```python
import jax
import jax.numpy as jnp
from jax import lax
from jax.sharding import PartitionSpec as P

QROWS = 128
CBLK = 256
K_CAND = 8


def slot_ranks(targets, count):
    table = (targets[:, None] == jnp.arange(count, dtype=jnp.int32)[None, :]).astype(jnp.int32)
    ranks = jnp.cumsum(table, axis=0) - 1
    return jnp.sum(ranks * table, axis=1)


def block_maxima(queries, table, picks):
    total, rows_n, width = queries.shape
    group = total // 8
    turns = total // group

    def one_turn(operands):
        query_part, pick_part = operands
        chosen = jnp.take(table, pick_part, axis=0)
        scores = jnp.einsum("gnd,gcd->gnc", query_part, chosen, preferred_element_type=jnp.float32)
        return jnp.max(scores, axis=2)

    result = lax.map(
        one_turn, (queries.reshape(turns, group, rows_n, width), picks.reshape(turns, group))
    )
    return result.reshape(total, rows_n) * width ** (-0.5)


def local(embeddings, coarse_ids, fine_ids, centroids, candidates):
    wide_count = lax.axis_size("wide")
    narrow_count = lax.axis_size("narrow")
    emb_rows, width = embeddings.shape
    cent_rows = centroids.shape[0]
    group_cents = cent_rows * narrow_count
    row_cap = (2 * emb_rows + wide_count - 1) // wide_count
    targets = coarse_ids[:, 0]
    row_pos = targets * row_cap + slot_ranks(targets, wide_count)
    send_rows = jnp.zeros((wide_count * row_cap, width), jnp.bfloat16).at[row_pos].set(embeddings)
    send_fine = jnp.full((wide_count * row_cap,), -1, jnp.int32).at[row_pos].set(fine_ids)
    recv_rows, recv_fine = (
        lax.all_to_all(
            send_rows.reshape(wide_count, row_cap, width),
            "wide",
            split_axis=0,
            concat_axis=0,
            tiled=True,
        ),
        lax.all_to_all(
            send_fine.reshape(wide_count, row_cap), "wide", split_axis=0, concat_axis=0, tiled=True
        ),
    )
    flat_rows = recv_rows.reshape(-1, width)
    flat_fine = recv_fine.reshape(-1)
    columns = jnp.arange(lax.axis_size("narrow") * cent_rows, dtype=jnp.int32)
    one_hot = (flat_fine[:, None] == columns[None, :]).astype(jnp.bfloat16)
    sums = lax.psum_scatter(
        lax.dot_general(
            one_hot, flat_rows, (((0,), (0,)), ((), ())), preferred_element_type=jnp.float32
        ).astype(jnp.bfloat16),
        "narrow",
        scatter_dimension=0,
        tiled=True,
    ).astype(jnp.float32)
    mixed = centroids.astype(jnp.float32) + sums
    scale_row = lax.rsqrt(jnp.mean(mixed * mixed, axis=1, keepdims=True) + 1e-06)
    new_centroids = (mixed * scale_row).astype(jnp.bfloat16)
    gathered = lax.all_gather(new_centroids, "narrow", axis=0, tiled=True)
    block_count = group_cents // CBLK
    block_table = gathered.reshape(block_count, CBLK, width)
    query_count = emb_rows // QROWS
    requests = query_count * K_CAND
    slot_cap = (2 * requests + wide_count - 1) // wide_count
    slot_total = wide_count * slot_cap
    wanted = candidates.reshape(-1)
    owner_group = wanted // block_count
    local_block = wanted - owner_group * block_count
    req_pos = owner_group * slot_cap + slot_ranks(owner_group, wide_count)
    req_query = jnp.arange(requests, dtype=jnp.int32) // K_CAND
    slot_query = jnp.zeros((slot_total,), jnp.int32).at[req_pos].set(req_query)
    slot_live = jnp.zeros((slot_total,), jnp.bool_).at[req_pos].set(True)
    slot_block = jnp.full((slot_total,), -1, jnp.int32).at[req_pos].set(local_block)
    query_blocks = embeddings.reshape(query_count, QROWS, width)
    send_queries = jnp.where(
        slot_live[:, None, None],
        jnp.take(query_blocks, slot_query, axis=0),
        jnp.zeros((), jnp.bfloat16),
    )
    ids_in = lax.all_to_all(
        slot_block.reshape(wide_count, slot_cap), "wide", split_axis=0, concat_axis=0, tiled=True
    )
    picks = jnp.clip(ids_in.reshape(-1), 0, block_count - 1)
    outgoing = jnp.take(block_table, picks, axis=0).reshape(wide_count, slot_cap, CBLK, width)
    fetched = lax.all_to_all(outgoing, "wide", split_axis=0, concat_axis=0, tiled=True)
    values = block_maxima(
        send_queries,
        fetched.reshape(slot_total, CBLK, width),
        jnp.arange(slot_total, dtype=jnp.int32),
    )
    per_request = jnp.take(values, req_pos, axis=0)
    best_score = jnp.max(per_request.reshape(query_count, K_CAND, QROWS), axis=1).reshape(emb_rows)
    return (new_centroids, best_score)


def solution(mesh):
    return jax.shard_map(
        local,
        mesh=mesh,
        in_specs=(
            P(("wide", "narrow"), None),
            P(("wide", "narrow"), None),
            P(("wide", "narrow")),
            P(("wide", "narrow"), None),
            P(("wide", "narrow"), None),
        ),
        out_specs=(P(("wide", "narrow"), None), P(("wide", "narrow"))),
        check_vma=False,
    )
```

profile of v0, /device:TPU:0, one launch (start us, length us, event | category | flops | bytes accessed | tf_op | source)
XLA Modules:
  0.0 827.4 jit_solution(12097914941548033054)
XLA Ops:
  10.7 3.2 scatter_custom_fusion
  13.9 7.3 all-to-all-start
  21.2 3.6 scatter_custom_fusion.1
  24.7 2.8 all-to-all-done
  27.5 39.5 %all_to_all.28 = bf16[8,128,768]{2,1,0:T(8,128)(2,1)S(1)} all-to-all(bf16[8,128,768]{2,1,0:T(8,128)(2,1)S(1)} %bitcast.70), channel_id=1, replica_groups=mesh['wide'=8,'narrow'=4] {'wide'}, dimensions={0} | all-to-all | bytes 3145728 | tf_op jit(solution)/shard_map/all_to_all | solution.py:46
  67.0 5.9 fusion.16
  73.0 37.0 %reduce-scatter.2.cloned.1.call-done = bf16[512,768]{1,0:T(8,128)(2,1)} async-done(((bf16[2048,768]{1,0:T(8,128)(2,1)}), bf16[512,768]{1,0:T(8,128)(2,1)}) %reduce-scatter.2.cloned.1.call-update) | async-done | bytes 786448 | tf_op jit(solution)/shard_map/reduce_scatter | solution.py:61
  115.1 11.8 %all_to_all.29 = s32[8,1,8]{2,1,0:T(1,128)S(1)} all-to-all(s32[8,1,8]{2,1,0:T(1,128)S(1)} %bitcast.76), channel_id=1, replica_groups=mesh['wide'=8,'narrow'=4] {'wide'}, dimensions={0} | all-to-all | bytes 512 | tf_op jit(solution)/shard_map/all_to_all | solution.py:93
  127.0 15.5 %all-gather.2.cloned.1.call-done = bf16[2048,768]{1,0:T(8,128)(2,1)} async-done(((bf16[512,768]{1,0:T(8,128)(2,1)}), bf16[2048,768]{1,0:T(8,128)(2,1)}) %all-gather.2.cloned.1.call-update) | async-done | bytes 3145744 | tf_op jit(solution)/shard_map/all_gather | solution.py:72
  142.5 12.1 %gather_fusion.2 = bf16[64,256,768]{2,1,0:T(8,128)(2,1)} fusion(bf16[8,256,768]{2,1,0:T(8,128)(2,1)} %bitcast.66, s32[1024]{0:T(1024)S(1)} %pad_clamp_fusion.2), kind=kCustom, calls=%fused_computation.2 | custom fusion | bytes 50331904 | tf_op jit(solution)/shard_map/jit(_take)/gather | solution.py:97
  154.6 21.3 %broadcast_select_fusion = bf16[8,8,256,768]{3,2,1,0:T(8,128)(2,1)} fusion(bf16[8,8,256,768]{3,2,1,0:T(8,128)(2,1)} %bitcast.68, pred[8,8]{1,0:T(8,128)(4,1)S(1)} %compare_and_fusion.1), kind=kLoop, calls=%fused_computation.25 | loop fusion | flops 12582912 | bytes 50331712 | tf_op jit(solution)/shard_map/jit(_take)/select_n | solution.py:97
  175.9 6.6 all-to-all-start.3
  184.3 7.0 gather_fusion.1
  191.4 11.1 %select_select_fusion = bf16[8,8,128,768]{3,2,1,0:T(8,128)(2,1)} fusion(bf16[8,8,128,768]{3,2,1,0:T(8,128)(2,1)} %bitcast.69, pred[8,8]{1,0:T(8,128)(4,1)S(1)} %broadcast_in_dim.109, pred[8,8]{1,0:T(8,128)(4,1)S(1)} %broadcast_in_dim.106), kind=kLoop, calls=%fused_computation.26 | loop fusion | flops 12582912 | bytes 25165952 | tf_op jit(solution)/shard_map/jit(_where)/select_n | solution.py:88
  202.5 523.1 %all-to-all-done.3 = bf16[8,8,256,768]{3,2,1,0:T(8,128)(2,1)} async-done(((bf16[8,8,256,768]{3,2,1,0:T(8,128)(2,1)}), bf16[8,8,256,768]{3,2,1,0:T(8,128)(2,1)}, u32[]{:S(2)}, u32[]{:S(2)}) %all-to-all-start.3) | async-done | bytes 25165856 | tf_op jit(solution)/shard_map/all_to_all | solution.py:98
  725.6 93.7 %while.10 = (s32[]{:T(128)}, f32[8,8,128]{2,1,0:T(8,128)S(1)}, bf16[8,8,128,768]{3,2,1,0:T(8,128)(2,1)}, s32[8,8]{1,0:T(8,128)S(1)}, bf16[64,256,768]{2,1,0:T(8,128)(2,1)}, /*index=5*/s32[]{:T(128)}) while((s32[]{:T(128)}, f32[8,8,128]{2,1,0:T(8,128)S(1)}, bf16[8,8,128,768]{3,2,1,0:T(8,128)(2,1)}, s32[8,8]{1,0:T(8,128)S(1)}, ...), condition=%wide.region_14.15_spmd, body=%wide.region_12.14_spmd.sunk | while | flops 404488256 | bytes 11027201 | solution.py:28
  725.7 8.9 %gather_fusion = bf16[8,256,768]{2,1,0:T(8,128)(2,1)S(1)} fusion(bf16[64,256,768]{2,1,0:T(8,128)(2,1)} %get-tuple-element.89, s32[1024]{0:T(1024)S(1)} %pad_clamp_fusion.5), kind=kCustom, calls=%fused_computation.clone.1 | custom fusion | bytes 6291488 | tf_op jit(solution)/shard_map/while/body/eval_jaxpr/jit(_take)/gather | solution.py:24
  737.4 8.9 %gather_fusion = bf16[8,256,768]{2,1,0:T(8,128)(2,1)S(1)} fusion(bf16[64,256,768]{2,1,0:T(8,128)(2,1)} %get-tuple-element.89, s32[1024]{0:T(1024)S(1)} %pad_clamp_fusion.5), kind=kCustom, calls=%fused_computation.clone.1 | custom fusion | bytes 6291488 | tf_op jit(solution)/shard_map/while/body/eval_jaxpr/jit(_take)/gather | solution.py:24
  749.1 8.9 %gather_fusion = bf16[8,256,768]{2,1,0:T(8,128)(2,1)S(1)} fusion(bf16[64,256,768]{2,1,0:T(8,128)(2,1)} %get-tuple-element.89, s32[1024]{0:T(1024)S(1)} %pad_clamp_fusion.5), kind=kCustom, calls=%fused_computation.clone.1 | custom fusion | bytes 6291488 | tf_op jit(solution)/shard_map/while/body/eval_jaxpr/jit(_take)/gather | solution.py:24
  760.8 8.9 %gather_fusion = bf16[8,256,768]{2,1,0:T(8,128)(2,1)S(1)} fusion(bf16[64,256,768]{2,1,0:T(8,128)(2,1)} %get-tuple-element.89, s32[1024]{0:T(1024)S(1)} %pad_clamp_fusion.5), kind=kCustom, calls=%fused_computation.clone.1 | custom fusion | bytes 6291488 | tf_op jit(solution)/shard_map/while/body/eval_jaxpr/jit(_take)/gather | solution.py:24
  772.5 8.9 %gather_fusion = bf16[8,256,768]{2,1,0:T(8,128)(2,1)S(1)} fusion(bf16[64,256,768]{2,1,0:T(8,128)(2,1)} %get-tuple-element.89, s32[1024]{0:T(1024)S(1)} %pad_clamp_fusion.5), kind=kCustom, calls=%fused_computation.clone.1 | custom fusion | bytes 6291488 | tf_op jit(solution)/shard_map/while/body/eval_jaxpr/jit(_take)/gather | solution.py:24
  784.2 8.9 %gather_fusion = bf16[8,256,768]{2,1,0:T(8,128)(2,1)S(1)} fusion(bf16[64,256,768]{2,1,0:T(8,128)(2,1)} %get-tuple-element.89, s32[1024]{0:T(1024)S(1)} %pad_clamp_fusion.5), kind=kCustom, calls=%fused_computation.clone.1 | custom fusion | bytes 6291488 | tf_op jit(solution)/shard_map/while/body/eval_jaxpr/jit(_take)/gather | solution.py:24
  795.9 8.9 %gather_fusion = bf16[8,256,768]{2,1,0:T(8,128)(2,1)S(1)} fusion(bf16[64,256,768]{2,1,0:T(8,128)(2,1)} %get-tuple-element.89, s32[1024]{0:T(1024)S(1)} %pad_clamp_fusion.5), kind=kCustom, calls=%fused_computation.clone.1 | custom fusion | bytes 6291488 | tf_op jit(solution)/shard_map/while/body/eval_jaxpr/jit(_take)/gather | solution.py:24
  807.7 8.9 %gather_fusion = bf16[8,256,768]{2,1,0:T(8,128)(2,1)S(1)} fusion(bf16[64,256,768]{2,1,0:T(8,128)(2,1)} %get-tuple-element.89, s32[1024]{0:T(1024)S(1)} %pad_clamp_fusion.5), kind=kCustom, calls=%fused_computation.clone.1 | custom fusion | bytes 6291488 | tf_op jit(solution)/shard_map/while/body/eval_jaxpr/jit(_take)/gather | solution.py:24
  (91 shorter events, 33.9 us)
Async XLA Ops:
  13.9 13.6 %all-to-all-start = ((s32[8,1,128]{2,1,0:T(1,128)}), s32[8,1,128]{2,1,0:T(1,128)S(1)}, u32[]{:S(2)}, u32[]{:S(2)}) async-start(s32[8,1,128]{2,1,0:T(1,128)} %bitcast.11), calls=%async_computation | async-start | bytes 8192 | tf_op jit(solution)/shard_map/all_to_all | solution.py:53
  21.1 88.9 %reduce-scatter.2.cloned.1.call-start = ((), (), s32[]{:S(2)}) async-start(), calls=%async_computation.5 | async-start | bytes 3932160 | tf_op jit(solution)/shard_map/reduce_scatter | solution.py:61
  72.9 37.1 %copy-start.1 = (bf16[512,768]{1,0:T(8,128)(2,1)S(1)}, bf16[512,768]{1,0:T(8,128)(2,1)}, u32[]{:S(2)}) copy-start(bf16[512,768]{1,0:T(8,128)(2,1)} %param.10) | copy-start | bytes 2359300
  72.9 40.9 %copy-start.2 = (s32[4,8]{1,0:T(4,128)S(1)}, s32[4,8]{1,0:T(4,128)}, u32[]{:S(2)}) copy-start(s32[4,8]{1,0:T(4,128)} %param.11) | copy-start | bytes 388
  72.9 69.5 %all-gather.2.cloned.1.call-start = ((), (), s32[]{:S(2)}) async-start(), calls=%async_computation.6 | async-start | bytes 3932160 | tf_op jit(solution)/shard_map/all_gather | solution.py:72
  175.9 8.4 %copy-start = (bf16[512,768]{1,0:T(8,128)(2,1)S(1)}, bf16[512,768]{1,0:T(8,128)(2,1)}, u32[]{:S(2)}) copy-start(bf16[512,768]{1,0:T(8,128)(2,1)} %param.7) | copy-start | bytes 2359300
  175.9 549.8 %all-to-all-start.3 = ((bf16[8,8,256,768]{3,2,1,0:T(8,128)(2,1)}), bf16[8,8,256,768]{3,2,1,0:T(8,128)(2,1)}, u32[]{:S(2)}, u32[]{:S(2)}) async-start(bf16[8,8,256,768]{3,2,1,0:T(8,128)(2,1)} %broadcast_select_fusion), calls=%async_computation.4 | async-start | bytes 50331648 | tf_op jit(solution)/shard_map/all_to_all | solution.py:98
Sparse Core Ops, SparseCore 0:
  73.1 36.9 reduce-scatter.1
  113.9 28.5 all-gather.1
where the time goes:
time: 829 us; the launch traced here: 827 us
  waiting for transfers between devices  579 us (70%)
  local copies, waits for them, and re-layouts  101 us (12%)
  blocking collectives  51.2 us (6%)
  other arithmetic  40.8 us (5%)
  matrix products  27.6 us (3%)
  between operations  14.2 us (2%)
  starting transfers between devices  13.9 us (2%)
    all_to_all x1, waiting for transfers between devices, local(): lax.all_to_all(outgoing, 'wide', split_axis=0, concat_axis=0, tiled=True)  523 us
    gather x8, local copies, waits for them, and re-layouts, one_turn(): chosen = jnp.take(table, pick_part, axis=0)  71.2 us
    all_to_all x1, blocking collectives, local(): lax.all_to_all(send_rows.reshape(wide_count, row_cap, width), 'wide', spl...  39.5 us
    reduce_scatter x1, waiting for transfers between devices, local(): lax.psum_scatter(lax.dot_general(one_hot, flat_rows, (((0,), (0,)), ((),...  37 us
    dot_general x8, matrix products, one_turn(): jnp.einsum('gnd,gcd->gnc', query_part, chosen, preferred_element_type=jnp...  21.7 us
    select_n x2, other arithmetic, local(): jnp.take(block_table, picks, axis=0)  21.3 us
  transfers between devices with their start and end apart: 4, of which 4 were waited for; matrix products, arithmetic and copies ran while one was open for 3% of the time, Pallas kernels for 0%

commit v1 on v0

--- a/solution.py
+++ b/solution.py
@@ -6,6 +6,17 @@
 QROWS = 128
 CBLK = 256
 K_CAND = 8
+
+
+def cut_along(array, dim, peers):
+    before, after = (array.shape[:dim], array.shape[dim + 1 :])
+    return jnp.moveaxis(array.reshape(*before, peers, -1, *after), dim, 0)
+
+
+def laid_out(tiles, dim):
+    shape = list(tiles.shape[1:])
+    shape[dim] *= tiles.shape[0]
+    return jnp.moveaxis(tiles, 0, dim).reshape(shape)
 
 
 def slot_ranks(targets, count):
@@ -95,7 +106,14 @@
     )
     picks = jnp.clip(ids_in.reshape(-1), 0, block_count - 1)
     outgoing = jnp.take(block_table, picks, axis=0).reshape(wide_count, slot_cap, CBLK, width)
-    fetched = lax.all_to_all(outgoing, "wide", split_axis=0, concat_axis=0, tiled=True)
+    size, position = (lax.axis_size("wide"), lax.axis_index("wide"))
+    blocks = cut_along(outgoing, 0, size)
+    done = [blocks[position]]
+    for turn in range(1, size):
+        sent = blocks[(position + turn) % size]
+        done.append(lax.ppermute(sent, "wide", [(i, (i + turn) % size) for i in range(size)]))
+    blocks = jnp.stack(done)[(position - jnp.arange(size)) % size]
+    fetched = laid_out(blocks, 0)
     values = block_maxima(
         send_queries,
         fetched.reshape(slot_total, CBLK, width),

time: 829 us -> 895 us (1.080)
  the two profiles are of different devices: /device:TPU:0 before, /device:TPU:26 now
where the time goes in v1:
time: 895 us; the launch traced here: 894 us
  waiting for transfers between devices  563 us (63%)
  local copies, waits for them, and re-layouts  168 us (19%)
  other arithmetic  61.8 us (7%)
  blocking collectives  39.8 us (4%)
  matrix products  27.6 us (3%)
  starting transfers between devices  19.1 us (2%)
  between operations  14.2 us (2%)
    ppermute x7, waiting for transfers between devices, local(): lax.ppermute(sent, 'wide', [(i, (i + turn) % size) for i in range(size)])  503 us
    gather x8, local copies, waits for them, and re-layouts, one_turn(): chosen = jnp.take(table, pick_part, axis=0)  71.3 us
    all_to_all x1, blocking collectives, local(): lax.all_to_all(send_rows.reshape(wide_count, row_cap, width), 'wide', spl...  39.8 us
    reduce_scatter x1, waiting for transfers between devices, local(): lax.psum_scatter(lax.dot_general(one_hot, flat_rows, (((0,), (0,)), ((),...  39 us
    gather x3, local copies, waits for them, and re-layouts, local(): blocks = jnp.stack(done)[(position - jnp.arange(size)) % size]  32.9 us
    dot_general x8, matrix products, one_turn(): jnp.einsum('gnd,gcd->gnc', query_part, chosen, preferred_element_type=jnp...  21.7 us
    select_n x2, other arithmetic, local(): jnp.take(block_table, picks, axis=0)  21.3 us
    unnamed x1, other arithmetic  20.4 us
  transfers between devices with their start and end apart: 11, of which 7 were waited for; matrix products, arithmetic and copies ran while one was open for 4% of the time, Pallas kernels for 0%

profile of v1, /device:TPU:26, one launch (start us, length us, event | category | flops | bytes accessed | tf_op | source)
XLA Modules:
  0.0 893.9 jit_solution(7042562999426527852)
XLA Ops:
  23.4 39.8 %all_to_all.23 = bf16[8,128,768]{2,1,0:T(8,128)(2,1)S(1)} all-to-all(bf16[8,128,768]{2,1,0:T(8,128)(2,1)S(1)} %bitcast.109), channel_id=1, replica_groups=mesh['wide'=8,'narrow'=4] {'wide'}, dimensions={0} | all-to-all | bytes 3145728 | tf_op jit(solution)/shard_map/all_to_all | solution.py:57
  69.3 39.0 %reduce-scatter.2.cloned.1.call-done = bf16[512,768]{1,0:T(8,128)(2,1)} async-done(((bf16[2048,768]{1,0:T(8,128)(2,1)}), bf16[512,768]{1,0:T(8,128)(2,1)}) %reduce-scatter.2.cloned.1.call-update) | async-done | bytes 786448 | tf_op jit(solution)/shard_map/reduce_scatter | solution.py:72
  122.4 18.4 %all-gather.2.cloned.1.call-done = bf16[2048,768]{1,0:T(8,128)(2,1)} async-done(((bf16[512,768]{1,0:T(8,128)(2,1)}), bf16[2048,768]{1,0:T(8,128)(2,1)}) %all-gather.2.cloned.1.call-update) | async-done | bytes 3145744 | tf_op jit(solution)/shard_map/all_gather | solution.py:83
  140.7 12.3 %gather_fusion.2 = bf16[64,256,768]{2,1,0:T(8,128)(2,1)} fusion(bf16[8,256,768]{2,1,0:T(8,128)(2,1)} %bitcast.102, s32[1024]{0:T(1024)S(1)} %pad_clamp_fusion.3), kind=kCustom, calls=%fused_computation.2 | custom fusion | bytes 50331904 | tf_op jit(solution)/shard_map/jit(_take)/gather | solution.py:108
  153.0 21.3 %broadcast_select_fusion = bf16[8,1,8,256,768]{4,3,2,0,1:T(8,128)(2,1)} fusion(bf16[8,1,8,256,768]{4,3,2,0,1:T(8,128)(2,1)} %bitcast.104, pred[8,8]{1,0:T(8,128)(4,1)S(1)} %compare_and_fusion.1), kind=kLoop, calls=%fused_computation.28 | loop fusion | flops 12582912 | bytes 50331712 | tf_op jit(solution)/shard_map/jit(_take)/select_n | solution.py:108
  174.3 17.2 %dynamic-slice_bitcast_fusion = (bf16[1,8,256,768]{3,2,1,0:T(8,128)(2,1)}, bf16[1,8,256,768]{3,2,1,0:T(8,128)(2,1)}, bf16[1,8,256,768]{3,2,1,0:T(8,128)(2,1)}, b...) fusion(bf16[8,1,8,256,768]{4,3,2,0,1:T(8,128)(2,1)} %broadcast_, ...), kind=kLoop, calls=%fused_computation.43 | loop fusion | bytes 50331680 | tf_op jit(solution)/shard_map/squeeze | solution.py:113
  207.2 55.0 %collective-permute-done = bf16[1,8,256,768]{3,2,1,0:T(8,128)(2,1)} collective-permute-done((bf16[1,8,256,768]{3,2,1,0:T(8,128)(2,1)}, bf16[1,8,256,768]{3,2,1,0:T(8,128)(2,1)}, u32[]{:S(2)}, u32[]{:S(2)}) %collective-permute-start) | collective-permute-done | bytes 3145760 | tf_op jit(solution)/shard_map/ppermute | solution.py:114
  262.7 67.1 %collective-permute-done.1 = bf16[1,8,256,768]{3,2,1,0:T(8,128)(2,1)} collective-permute-done((bf16[1,8,256,768]{3,2,1,0:T(8,128)(2,1)}, bf16[1,8,256,768]{3,2,1,0:T(8,128)(2,1)}, u32[]{:S(2)}, u32[]{:S(2)}) %collective-permute-start.1) | collective-permute-done | bytes 3145760 | tf_op jit(solution)/shard_map/ppermute | solution.py:114
  329.8 11.7 %select_select_fusion = bf16[8,8,128,768]{3,2,1,0:T(8,128)(2,1)} fusion(bf16[8,8,128,768]{3,2,1,0:T(8,128)(2,1)} %bitcast.106, pred[8,8]{1,0:T(8,128)(4,1)S(1)} %broadcast_in_dim.110, pred[8,8]{1,0:T(8,128)(4,1)S(1)} %broadcast_in_dim.107), kind=kLoop, calls=%fused_computation.31 | loop fusion | flops 12582912 | bytes 25165952 | tf_op jit(solution)/shard_map/jit(_where)/select_n | solution.py:99
  350.6 45.2 %collective-permute-done.2 = bf16[1,8,256,768]{3,2,1,0:T(8,128)(2,1)} collective-permute-done((bf16[1,8,256,768]{3,2,1,0:T(8,128)(2,1)}, bf16[1,8,256,768]{3,2,1,0:T(8,128)(2,1)}, u32[]{:S(2)}, u32[]{:S(2)}) %collective-permute-start.2) | collective-permute-done | bytes 3145760 | tf_op jit(solution)/shard_map/ppermute | solution.py:114
  397.9 336.1 %collective-permute-done.3 = bf16[1,8,256,768]{3,2,1,0:T(8,128)(2,1)} collective-permute-done((bf16[1,8,256,768]{3,2,1,0:T(8,128)(2,1)}, bf16[1,8,256,768]{3,2,1,0:T(8,128)(2,1)}, u32[]{:S(2)}, u32[]{:S(2)}) %collective-permute-start.3) | collective-permute-done | bytes 3145760 | tf_op jit(solution)/shard_map/ppermute | solution.py:114
  738.8 10.2 %slice_bitcast_fusion.1 = (bf16[8,8,256,384]{3,2,1,0:T(8,128)(2,1)}, bf16[8,8,256,384]{3,2,1,0:T(8,128)(2,1)}) fusion(bf16[8,1,8,256,768]{4,3,2,0,1:T(8,128)(2,1)S(1)} %bitcast_dynamic-update-slice_fusion.1), kind=kLoop, calls=%fused_computation.30 | loop fusion | bytes 50331648 | tf_op jit(solution)/shard_map/gather | solution.py:115
  748.9 11.3 %gather_fusion.4 = bf16[8,8,256,384]{3,2,1,0:T(8,128)(2,1)} fusion(bf16[8,8,256,384]{3,2,1,0:T(8,128)(2,1)} %get-tuple-element.42, s32[1024]{0:T(1024)S(1)} %pad_clamp_fusion.2), kind=kCustom, calls=%fused_computation.4 | custom fusion | bytes 25165856 | tf_op jit(solution)/shard_map/gather | solution.py:115
  760.3 11.4 %gather_fusion.5 = bf16[8,8,256,384]{3,2,1,0:T(8,128)(2,1)} fusion(bf16[8,8,256,384]{3,2,1,0:T(8,128)(2,1)} %get-tuple-element.43, s32[1024]{0:T(1024)S(1)} %pad_clamp_fusion.2), kind=kCustom, calls=%fused_computation.5 | custom fusion | bytes 25165856 | tf_op jit(solution)/shard_map/gather | solution.py:115
  771.6 20.4 %pad_maximum_fusion = bf16[8,1,8,256,768]{4,3,2,0,1:T(8,128)(2,1)} fusion(bf16[8,1,8,256,384]{4,3,2,0,1:T(8,128)(2,1)} %bitcast.108, bf16[8,1,8,256,384]{4,3,2,0,1:T(8,128)(2,1)} %bitcast.107), kind=kLoop, calls=%fused_computation.27 | loop fusion | flops 50331648 | bytes 50331648
  792.1 93.7 %while.10 = (s32[]{:T(128)}, f32[8,8,128]{2,1,0:T(8,128)S(1)}, bf16[8,8,128,768]{3,2,1,0:T(8,128)(2,1)}, s32[8,8]{1,0:T(8,128)S(1)}, bf16[64,256,768]{2,1,0:T(8,128)(2,1)}, /*index=5*/s32[]{:T(128)}) while((s32[]{:T(128)}, f32[8,8,128]{2,1,0:T(8,128)S(1)}, bf16[8,8,128,768]{3,2,1,0:T(8,128)(2,1)}, s32[8,8]{1,0:T(8,128)S(1)}, ...), condition=%wide.region_14.15_spmd, body=%wide.region_12.14_spmd.sunk | while | flops 404488256 | bytes 11027201 | solution.py:39
  792.1 8.9 gather_fusion
  803.8 8.9 gather_fusion
  815.5 8.9 gather_fusion
  827.2 8.9 gather_fusion
  838.9 8.9 gather_fusion
  850.7 8.9 gather_fusion
  862.4 8.9 gather_fusion
  874.1 8.9 gather_fusion
  (119 shorter events, 91.6 us)
Async XLA Ops:
  13.9 9.6 %all-to-all-start = ((s32[8,1,128]{2,1,0:T(1,128)}), s32[8,1,128]{2,1,0:T(1,128)S(1)}, u32[]{:S(2)}, u32[]{:S(2)}) async-start(s32[8,1,128]{2,1,0:T(1,128)} %bitcast.11), calls=%async_computation | async-start | bytes 8192 | tf_op jit(solution)/shard_map/all_to_all | solution.py:64
  19.9 88.4 %reduce-scatter.2.cloned.1.call-start = ((), (), s32[]{:S(2)}) async-start(), calls=%async_computation.4 | async-start | bytes 3932160 | tf_op jit(solution)/shard_map/reduce_scatter | solution.py:72
  63.3 45.0 %copy-start.2 = (bf16[512,768]{1,0:T(8,128)(2,1)S(1)}, bf16[512,768]{1,0:T(8,128)(2,1)}, u32[]{:S(2)}) copy-start(bf16[512,768]{1,0:T(8,128)(2,1)} %param.10) | copy-start | bytes 2359300
  63.3 48.8 %copy-start.3 = (s32[4,8]{1,0:T(4,128)S(1)}, s32[4,8]{1,0:T(4,128)}, u32[]{:S(2)}) copy-start(s32[4,8]{1,0:T(4,128)} %param.11) | copy-start | bytes 388
  69.2 71.5 %all-gather.2.cloned.1.call-start = ((), (), s32[]{:S(2)}) async-start(), calls=%async_computation.5 | async-start | bytes 3932160 | tf_op jit(solution)/shard_map/all_gather | solution.py:83
  113.9 8.3 all-to-all-start.2
  174.3 25.6 %copy-start = (bf16[512,768]{1,0:T(8,128)(2,1)S(1)}, bf16[512,768]{1,0:T(8,128)(2,1)}, u32[]{:S(2)}) copy-start(bf16[512,768]{1,0:T(8,128)(2,1)} %param.7) | copy-start | bytes 2359300
  191.5 70.7 %collective-permute-start = (bf16[1,8,256,768]{3,2,1,0:T(8,128)(2,1)}, bf16[1,8,256,768]{3,2,1,0:T(8,128)(2,1)}, u32[]{:S(2)}, u32[]{:S(2)}) collective-permute-start(bf16[1,8,256,768]{3,2,1,0:T(8,128)(2,1)} %get-tuple-element.50), channel_id=1, source_target_pairs={{0,4},{4,8},{8,12},{12,16},{16,20},{20,24},{24,28},{28,0},{1,5},{5... | collective-permute-start | bytes 9437192 | tf_op jit(solution)/shard_map/ppermute | solution.py:114
  192.1 137.7 %collective-permute-start.1 = (bf16[1,8,256,768]{3,2,1,0:T(8,128)(2,1)}, bf16[1,8,256,768]{3,2,1,0:T(8,128)(2,1)}, u32[]{:S(2)}, u32[]{:S(2)}) collective-permute-start(bf16[1,8,256,768]{3,2,1,0:T(8,128)(2,1)} %get-tuple-element.49), channel_id=1, source_target_pairs={{0,8},{4,12},{8,16},{12,20},{16,24},{20,28},{24,0},{28,4},{1,9},{5... | collective-permute-start | bytes 9437192 | tf_op jit(solution)/shard_map/ppermute | solution.py:114
  193.7 202.1 %collective-permute-start.2 = (bf16[1,8,256,768]{3,2,1,0:T(8,128)(2,1)}, bf16[1,8,256,768]{3,2,1,0:T(8,128)(2,1)}, u32[]{:S(2)}, u32[]{:S(2)}) collective-permute-start(bf16[1,8,256,768]{3,2,1,0:T(8,128)(2,1)} %get-tuple-element.48), channel_id=1, source_target_pairs={{0,12},{4,16},{8,20},{12,24},{16,28},{20,0},{24,4},{28,8},{1,13},{... | collective-permute-start | bytes 9437192 | tf_op jit(solution)/shard_map/ppermute | solution.py:114
  195.7 538.3 %collective-permute-start.3 = (bf16[1,8,256,768]{3,2,1,0:T(8,128)(2,1)}, bf16[1,8,256,768]{3,2,1,0:T(8,128)(2,1)}, u32[]{:S(2)}, u32[]{:S(2)}) collective-permute-start(bf16[1,8,256,768]{3,2,1,0:T(8,128)(2,1)} %get-tuple-element.47), channel_id=1, source_target_pairs={{0,16},{4,20},{8,24},{12,28},{16,0},{20,4},{24,8},{28,12},{1,17},{... | collective-permute-start | bytes 9437192 | tf_op jit(solution)/shard_map/ppermute | solution.py:114
  197.3 538.8 %collective-permute-start.4 = (bf16[1,8,256,768]{3,2,1,0:T(8,128)(2,1)}, bf16[1,8,256,768]{3,2,1,0:T(8,128)(2,1)}, u32[]{:S(2)}, u32[]{:S(2)}) collective-permute-start(bf16[1,8,256,768]{3,2,1,0:T(8,128)(2,1)} %get-tuple-element.46), channel_id=1, source_target_pairs={{0,20},{4,24},{8,28},{12,0},{16,4},{20,8},{24,12},{28,16},{1,21},{... | collective-permute-start | bytes 9437192 | tf_op jit(solution)/shard_map/ppermute | solution.py:114
  262.2 476.1 %collective-permute-start.5 = (bf16[1,8,256,768]{3,2,1,0:T(8,128)(2,1)}, bf16[1,8,256,768]{3,2,1,0:T(8,128)(2,1)S(1)}, u32[]{:S(2)}, u32[]{:S(2)}) collective-permute-start(bf16[1,8,256,768]{3,2,1,0:T(8,128)(2,1)} %get-tuple-element.45), channel_id=1, source_target_pairs={{0,24},{4,28},{8,0},{12,4},{16,8},{20,12},{24,16},{28,20},{1,25},{... | collective-permute-start | bytes 9437192 | tf_op jit(solution)/shard_map/ppermute | solution.py:114
  329.8 408.7 %collective-permute-start.6 = (bf16[1,8,256,768]{3,2,1,0:T(8,128)(2,1)}, bf16[1,8,256,768]{3,2,1,0:T(8,128)(2,1)S(1)}, u32[]{:S(2)}, u32[]{:S(2)}) collective-permute-start(bf16[1,8,256,768]{3,2,1,0:T(8,128)(2,1)} %get-tuple-element.44), channel_id=1, source_target_pairs={{0,28},{4,0},{8,4},{12,8},{16,12},{20,16},{24,20},{28,24},{1,29},{... | collective-permute-start | bytes 9437192 | tf_op jit(solution)/shard_map/ppermute | solution.py:114
  329.8 16.6 %copy-start.1 = (bf16[8,1,8,256,768]{4,3,2,0,1:T(8,128)(2,1)S(1)}, bf16[8,1,8,256,768]{4,3,2,0,1:T(8,128)(2,1)}, u32[]{:S(2)}) copy-start(bf16[8,1,8,256,768]{4,3,2,0,1:T(8,128)(2,1)} %get-tuple-element.51) | copy-start | bytes 75497472
Sparse Core Ops, SparseCore 0:
  69.3 38.8 reduce-scatter.1
  112.2 28.5 all-gather.1
